TPU v7x, 256 devices: a whole 4x4x8 slice. The times are simulated.
256 devices in a mesh: member: 16 (over z, core), region: 16 (over y, x).
Axes of the slice: x: 4, y: 4, z: 8, core: 2. Of those that a mesh axis runs over, the one named last changes fastest.
Arguments:
- prior_states: bfloat16 [512, 524288], P('member', 'region'), may hold values from -6 to 6
- measured_values: bfloat16 [65536], P('region'), may hold values from -12 to 12
- measurement_precision: bfloat16 [65536], P('region'), may hold values from 0.5 to 4
- measured_subgrid_line: int32 [65536], P('region'), may hold values from 0 to 32767, as said below
- neighbour_measurement_lookup: int32 [16, 16, 1024], P('region'), may hold values from 0 to 12287, as said below
- active_entries_tally: int32 [16, 16], P('region', 'member'), may hold values from 512 to 1024, as said below
- distance_tier: int32 [16, 16, 1024], P('region', 'member'), may hold values from 0 to 8
- eastward_weight_share: int32 [16, 16, 2048], P('region', 'member'), may hold values from 0 to 8
Outputs:
- analysis: bfloat16 [512, 524288], P('member', 'region')
Inputs may be any that keep to these rules, and one draw needn't show every extreme that they name: `neighbour_measurement_lookup`: for coarse point (s, p) the live and dead slots name distinct observations, all in blocks p-1, p, p+1 (each block 256 observations of a sector, in order) of sectors s-1, s, s+1; blocks outside 0 to 15 are never named. `measured_subgrid_line`: observation o of a sector measures a row of its block: from ((o % 4096) // 256) * 2048 to that plus 2048 - 1. `active_entries_tally`: some coarse point has all 1024 slots live.
All inputs are finite; a program needn't handle non-finite values.
Results may differ from a plain program's by a relative error of at most 0.019.
Values may be sent and summed in bfloat16 or wider, within the bound.
A program may use at most 64 MiB of HBM per device.

v0:
```python
import jax
import jax.numpy as jnp
from jax import lax
from jax.sharding import PartitionSpec as P

ITERS = 6


def with_halo(block, sides, width):
    for axis, dim in sides:
        count = lax.axis_size(axis)
        forward = [(i, i + 1) for i in range(count - 1)]
        forward.append((count - 1, 0))
        backward = [(target, source) for source, target in forward]
        low = lax.ppermute(
            lax.slice_in_dim(block, block.shape[dim] - width, None, axis=dim), axis, forward
        )
        high = lax.ppermute(lax.slice_in_dim(block, 0, width, axis=dim), axis, backward)
        block = jnp.concatenate([low, block, high], axis=dim)
    return block


def in_blocks(value, dim, size):
    before, after = (value.shape[:dim], value.shape[dim + 1 :])
    return jnp.moveaxis(value.reshape(*before, size, -1, *after), dim, 0)


def edges_of(length, count):
    step = length // count
    if step >= 8:
        step -= step % 8
    return [step * k for k in range(1, count)]


def joined_along(parts, dim):
    parts = jnp.moveaxis(parts, 0, dim)
    shape = parts.shape
    return parts.reshape(*shape[:dim], shape[dim] * shape[dim + 1], *shape[dim + 2 :])


def exchange_in_pieces(value, axis, pieces, split_dim, concat_dim):
    parts = in_blocks(value, split_dim, lax.axis_size(axis))
    widest = max(range(1, max(2, parts.ndim - 1)), key=lambda d: parts.shape[d])
    outs = []
    for slab in jnp.split(parts, edges_of(parts.shape[widest], pieces), axis=widest):
        if slab.size:
            outs.append(lax.all_to_all(slab, axis, split_axis=0, concat_axis=0, tiled=True))
    return joined_along(jnp.concatenate(outs, axis=widest), concat_dim)


def shifted(value, axis, steps):
    count = lax.axis_size(axis)
    pairs = [(source, (source + steps) % count) for source in range(count)]
    return lax.ppermute(value, axis, pairs)


def transform(chosen, obs_val, obs_w, count, dist):
    ensemble_dimension = chosen.shape[0]
    slots = chosen.shape[1]
    values = chosen.astype(jnp.float32)
    ybar = jnp.mean(values, axis=0)
    pert = (values - ybar).astype(jnp.bfloat16)
    live = (jnp.arange(slots, dtype=jnp.int32) < count).astype(jnp.float32)
    wts = obs_w.astype(jnp.float32) * 2.0 / (2.0 + dist.astype(jnp.float32)) * live
    weighted = pert.astype(jnp.float32) * wts
    gram = lax.dot_general(
        weighted.astype(jnp.bfloat16),
        pert,
        (((1,), (1,)), ((), ())),
        preferred_element_type=jnp.float32,
    )
    identity = jnp.eye(ensemble_dimension, dtype=jnp.float32)
    amat = gram + (ensemble_dimension - 1.0) * identity
    norm = jnp.sqrt(jnp.sum(amat * amat))
    gvec = jnp.dot(weighted, obs_val.astype(jnp.float32) - ybar)
    zmat = (amat / norm).astype(jnp.bfloat16)
    ymat = identity.astype(jnp.bfloat16)
    for step in range(ITERS):
        product = jnp.dot(zmat, ymat, preferred_element_type=jnp.float32)
        tmat = (1.5 * identity - 0.5 * product).astype(jnp.bfloat16)
        ynext = jnp.dot(ymat, tmat, preferred_element_type=jnp.float32).astype(jnp.bfloat16)
        zmat = jnp.dot(tmat, zmat, preferred_element_type=jnp.float32).astype(jnp.bfloat16)
        ymat = ynext
    isq = ymat.astype(jnp.float32) / jnp.sqrt(norm)
    wbar = jnp.dot(isq, jnp.dot(isq, gvec))
    return (jnp.sqrt(ensemble_dimension - 1.0) * isq + wbar[:, None]).astype(jnp.bfloat16)


def update(vertical_dimension, weights, eastern, level):
    values = vertical_dimension.astype(jnp.float32)
    xbar = jnp.mean(values, axis=0)
    centred = (values - xbar).astype(jnp.bfloat16)
    dims = (((0,), (0,)), ((), ()))
    own_term = lax.dot_general(weights, centred, dims, preferred_element_type=jnp.float32)
    east_term = lax.dot_general(eastern, centred, dims, preferred_element_type=jnp.float32)
    share = level.astype(jnp.float32) / 8.0
    return (xbar + (1.0 - share) * own_term + share * east_term).astype(jnp.bfloat16)


def local(
    prior_states,
    measured_values,
    measurement_precision,
    measured_subgrid_line,
    neighbour_measurement_lookup,
    active_entries_tally,
    distance_tier,
    eastward_weight_share,
):
    my_band = lax.axis_index("member")
    latitude_swaths = lax.axis_size("member")
    ensemble_dimension = prior_states.shape[0] * latitude_swaths
    obs_tile = measured_values.shape[0]
    obs_block = obs_tile // latitude_swaths
    mapped_dimension = jnp.take(prior_states, measured_subgrid_line, axis=1)
    paired = jnp.stack((measured_values, measurement_precision))
    own_list = lax.dynamic_index_in_dim(neighbour_measurement_lookup[0], my_band, 0, keepdims=False)
    banded = lax.all_to_all(mapped_dimension, "member", split_axis=1, concat_axis=0, tiled=True)
    own_pair = lax.dynamic_slice_in_dim(paired, my_band * obs_block, obs_block, 1)
    blocks, pairs = (
        with_halo(banded[None, None], (("member", 1), ("region", 0)), 1),
        with_halo(own_pair[None, None], (("member", 1), ("region", 0)), 1),
    )
    side = own_list // obs_tile
    within = own_list % obs_tile
    slot_block = side * 3 + within // obs_block - my_band + 1
    inside = within % obs_block
    blocks = blocks.reshape(9, ensemble_dimension, obs_block)
    pairs = pairs.reshape(9, 2, obs_block)
    chosen = blocks[slot_block, :, inside].T
    chosen_pair = pairs[slot_block, :, inside].T
    weights = transform(
        chosen, chosen_pair[0], chosen_pair[1], active_entries_tally[0, 0], distance_tier[0, 0]
    )
    vertical_dimension = exchange_in_pieces(prior_states, "member", 2, 1, 0)
    eastern = shifted(weights, "region", -1)
    result = update(vertical_dimension, weights, eastern, eastward_weight_share[0, 0])
    return lax.all_to_all(result, "member", split_axis=0, concat_axis=1, tiled=True)


def solution(mesh):
    in_specs = (
        P("member", "region"),
        P("region"),
        P("region"),
        P("region"),
        P("region", None, None),
        P("region", "member"),
        P("region", "member", None),
        P("region", "member", None),
    )
    out_specs = P("member", "region")
    return jax.shard_map(local, mesh=mesh, in_specs=in_specs, out_specs=out_specs, check_vma=False)
```

profile of v0, /device:TPU:1, one launch (start us, length us, event | category | flops | bytes accessed | tf_op | source)
XLA Modules:
  0.0 234.9 jit_solution(6443221171064780517)
XLA Ops:
  1.5 3.2 %collective-permute-start.5 = (bf16[1,1,2,256]{3,2,1,0:T(2,128)(2,1)S(1)}, bf16[1,1,2,256]{3,2,1,0:T(2,128)(2,1)S(1)}, u32[]{:S(2)}, u32[]{:S(2)}) collective-permute-start(bf16[1,1,2,256]{3,2,1,0:T(2,128)(2,1)S(1)} %fusion.36), channel_id=1, source_target_pairs={{16,0},{32,16},{48,32},{64,48},{80,64},{96,80},{112,96},{128,112},... | collective-permute-start | bytes 3080 | tf_op jit(solution)/shard_map/ppermute | solution.py:18
  6.2 7.4 %copy.19 = bf16[32,32768]{0,1:T(8,128)(2,1)} copy(bf16[32,32768]{1,0:T(8,128)(2,1)} %param.8) | data formatting | bytes 4194304 | tf_op args[0]
  13.6 15.6 %gather_fusion = bf16[4096,32]{1,0:T(8,128)(2,1)S(1)} fusion(bf16[32,32768]{0,1:T(8,128)(2,1)} %copy.19, s32[4096]{0:T(1024)S(1)} %fusion.30), kind=kCustom, calls=%fused_computation | custom fusion | bytes 540672 | tf_op jit(solution)/shard_map/jit(_take)/gather | solution.py:115
  30.3 7.9 %all-to-all-start.2 = ((bf16[32,16,256]{2,0,1:T(8,128)(2,1)}), bf16[32,16,256]{2,0,1:T(8,128)(2,1)S(1)}, u32[]{:S(2)}, u32[]{:S(2)}) async-start(bf16[32,16,256]{2,0,1:T(8,128)(2,1)} %broadcast_select_fusion), calls=%async_computation.2 | async-start | bytes 524288 | tf_op jit(solution)/shard_map/all_to_all | solution.py:118
  38.4 1.4 fusion.38
  39.9 10.1 %all-to-all-done.2 = bf16[32,16,256]{2,0,1:T(8,128)(2,1)S(1)} async-done(((bf16[32,16,256]{2,0,1:T(8,128)(2,1)}), bf16[32,16,256]{2,0,1:T(8,128)(2,1)S(1)}, u32[]{:S(2)}, u32[]{:S(2)}) %all-to-all-start.2) | async-done | bytes 262176 | tf_op jit(solution)/shard_map/all_to_all | solution.py:118
  50.0 4.2 %all-to-all-start.1 = ((bf16[16,16,2048]{2,1,0:T(8,128)(2,1)}), bf16[16,16,2048]{2,1,0:T(8,128)(2,1)}, u32[]{:S(2)}, u32[]{:S(2)}) async-start(bf16[16,16,2048]{2,1,0:T(8,128)(2,1)} %get-tuple-element.8), calls=%async_computation.1 | async-start | bytes 2097152 | tf_op jit(solution)/shard_map/all_to_all | solution.py:47
  54.2 1.7 collective-permute-start
  56.0 25.8 %collective-permute-done.1 = bf16[1,1,512,256]{3,2,1,0:T(8,128)(2,1)S(1)} collective-permute-done((bf16[1,1,512,256]{3,2,1,0:T(8,128)(2,1)S(1)}, bf16[1,1,512,256]{3,2,1,0:T(8,128)(2,1)S(1)}, u32[]{:S(2)}, u32[]{:S(2)}) %collective-permute-start.1) | collective-permute-done | bytes 262176 | tf_op jit(solution)/shard_map/ppermute | solution.py:18
  81.8 1.0 pad_maximum_fusion.1
  82.7 4.9 %collective-permute-start.3 = (bf16[1,3,512,256]{3,2,1,0:T(8,128)(2,1)}, bf16[1,3,512,256]{3,2,1,0:T(8,128)(2,1)S(1)}, u32[]{:S(2)}, u32[]{:S(2)}) collective-permute-start(bf16[1,3,512,256]{3,2,1,0:T(8,128)(2,1)} %pad_maximum_fusion.1), channel_id=1, source_target_pairs={{1,0},{2,1},{3,2},{4,3},{5,4},{6,5},{7,6},{8,7},{9,8},{10,9},{11,1... | collective-permute-start | bytes 2359304 | tf_op jit(solution)/shard_map/ppermute | solution.py:18
  87.7 4.9 %collective-permute-start.7 = (bf16[1,3,2,256]{3,2,1,0:T(2,128)(2,1)S(1)}, bf16[1,3,2,256]{3,2,1,0:T(2,128)(2,1)S(1)}, u32[]{:S(2)}, u32[]{:S(2)}) collective-permute-start(bf16[1,3,2,256]{3,2,1,0:T(2,128)(2,1)S(1)} %pad_maximum_fusion.3), channel_id=1, source_target_pairs={{1,0},{2,1},{3,2},{4,3},{5,4},{6,5},{7,6},{8,7},{9,8},{10,9},{11,1... | collective-permute-start | bytes 9224 | tf_op jit(solution)/shard_map/ppermute | solution.py:18
  94.3 8.9 %collective-permute-done.7 = bf16[1,3,2,256]{3,2,1,0:T(2,128)(2,1)S(1)} collective-permute-done((bf16[1,3,2,256]{3,2,1,0:T(2,128)(2,1)S(1)}, bf16[1,3,2,256]{3,2,1,0:T(2,128)(2,1)S(1)}, u32[]{:S(2)}, u32[]{:S(2)}) %collective-permute-start.7) | collective-permute-done | bytes 3104 | tf_op jit(solution)/shard_map/ppermute | solution.py:18
  103.2 5.3 %collective-permute-done.6 = bf16[1,3,2,256]{3,2,1,0:T(2,128)(2,1)S(1)} collective-permute-done((bf16[1,3,2,256]{3,2,1,0:T(2,128)(2,1)S(1)}, bf16[1,3,2,256]{3,2,1,0:T(2,128)(2,1)S(1)}, u32[]{:S(2)}, u32[]{:S(2)}) %collective-permute-start.6) | collective-permute-done | bytes 3104 | tf_op jit(solution)/shard_map/ppermute | solution.py:15
  108.9 5.8 %gather_fusion.2 = bf16[1024,2]{1,0:T(8,128)(2,1)S(1)} fusion(bf16[9,2,256]{1,2,0:T(8,128)(2,1)S(1)} %bitcast.112, s32[1024]{0:T(1024)S(1)} %bitcast.109), kind=kCustom, calls=%fused_computation.2 | custom fusion | bytes 16384 | tf_op jit(solution)/shard_map/gather | solution.py:131
  115.2 2.6 %pad_maximum_fusion = bf16[3,3,512,256]{3,2,1,0:T(8,128)(2,1)} fusion(bf16[1,3,512,256]{3,2,1,0:T(8,128)(2,1)S(1)} %collective-permute-done.3, bf16[1,1,512,256]{3,2,1,0:T(8,128)(2,1)S(1)} %collective-permute-done.1, bf16[1,1,512,256]{3,2,1,0:T(8,128)(2,1)S(1)} %bitcast.119, bf16[1,1,512,256]{3,2,1,0:T(8,128)(2,1)S(1)} %collective-permute-done, ...), kind=kLoop, calls=%fused_computation.14 | loop fusion | flops 4718592 | bytes 4718592 | tf_op jit(solution)/shard_map/concatenate | solution.py:19
  117.7 2.8 %copy.21 = bf16[3,3,512,256]{2,3,1,0:T(8,128)(2,1)S(1)} copy(bf16[3,3,512,256]{3,2,1,0:T(8,128)(2,1)} %pad_maximum_fusion) | data formatting | bytes 4718592 | tf_op jit(solution)/shard_map/concatenate | solution.py:19
  120.6 7.3 %gather_fusion.1 = bf16[1024,512]{1,0:T(8,128)(2,1)S(1)} fusion(bf16[9,512,256]{1,2,0:T(8,128)(2,1)S(1)} %bitcast.111, s32[1024]{0:T(1024)S(1)} %bitcast.110), kind=kCustom, calls=%fused_computation.1 | custom fusion | bytes 2105344 | tf_op jit(solution)/shard_map/gather | solution.py:130
  128.1 1.9 multiply_reduce_fusion
  136.0 8.5 %all-to-all-start = ((bf16[16,16,2048]{2,1,0:T(8,128)(2,1)}), bf16[16,16,2048]{2,1,0:T(8,128)(2,1)S(1)}, u32[]{:S(2)}, u32[]{:S(2)}) async-start(bf16[16,16,2048]{2,1,0:T(8,128)(2,1)} %get-tuple-element.7), calls=%async_computation | async-start | bytes 2097152 | tf_op jit(solution)/shard_map/all_to_all | solution.py:47
  144.5 2.3 convolution_convert_fusion.3
  146.8 1.5 fusion.12
  149.2 1.2 convolution_convert_fusion.2
  150.4 2.7 %fusion.13 = bf16[512,512]{1,0:T(8,128)(2,1)} fusion(bf16[512,512]{1,0:T(8,128)(2,1)} %convolution_convert_fusion.2, bf16[512,512]{1,0:T(8,128)(2,1)} %copy-done.3, bf16[512,512]{1,0:T(8,128)(2,1)S(1)} %copy-done.2), kind=kOutput, calls=%fused_computation.48 | convolution fusion | flops 538443776 | bytes 2097152 | tf_op jit(solution)/shard_map/dot_general | solution.py:79
  153.1 1.6 fusion.7
  156.2 16.3 %all-to-all-done = bf16[16,16,2048]{2,1,0:T(8,128)(2,1)S(1)} async-done(((bf16[16,16,2048]{2,1,0:T(8,128)(2,1)}), bf16[16,16,2048]{2,1,0:T(8,128)(2,1)S(1)}, u32[]{:S(2)}, u32[]{:S(2)}) %all-to-all-start) | async-done | bytes 1048608 | tf_op jit(solution)/shard_map/all_to_all | solution.py:47
  172.4 1.6 fusion.29
  174.0 1.7 maximum_convert_fusion
  176.3 1.3 fusion.40
  177.6 1.5 add_convert_fusion
  179.1 54.3 %all_to_all.42 = bf16[16,32,2048]{2,1,0:T(8,128)(2,1)S(1)} all-to-all(bf16[16,32,2048]{2,1,0:T(8,128)(2,1)S(1)} %bitcast.121), channel_id=1, replica_groups=mesh['member'=16,'region'=16] {'member'}, dimensions={0} | all-to-all | bytes 4194304 | tf_op jit(solution)/shard_map/all_to_all | solution.py:138
  233.4 1.5 copy.26
  (60 shorter events, 14.2 us)
Async XLA Ops:
  1.5 86.2 %collective-permute-start.5 = (bf16[1,1,2,256]{3,2,1,0:T(2,128)(2,1)S(1)}, bf16[1,1,2,256]{3,2,1,0:T(2,128)(2,1)S(1)}, u32[]{:S(2)}, u32[]{:S(2)}) collective-permute-start(bf16[1,1,2,256]{3,2,1,0:T(2,128)(2,1)S(1)} %fusion.36), channel_id=1, source_target_pairs={{16,0},{32,16},{48,32},{64,48},{80,64},{96,80},{112,96},{128,112},... | collective-permute-start | bytes 3080 | tf_op jit(solution)/shard_map/ppermute | solution.py:18
  4.8 83.0 %collective-permute-start.4 = (bf16[1,1,2,256]{3,2,1,0:T(2,128)(2,1)S(1)}, bf16[1,1,2,256]{3,2,1,0:T(2,128)(2,1)S(1)}, u32[]{:S(2)}, u32[]{:S(2)}) collective-permute-start(bf16[1,1,2,256]{3,2,1,0:T(2,128)(2,1)S(1)} %fusion.36), channel_id=1, source_target_pairs={{0,16},{16,32},{32,48},{48,64},{64,80},{80,96},{96,112},{112,128},... | collective-permute-start | bytes 3080 | tf_op jit(solution)/shard_map/ppermute | solution.py:15
  13.6 24.7 %copy-start = (bf16[32,32768]{1,0:T(8,128)(2,1)S(1)}, bf16[32,32768]{1,0:T(8,128)(2,1)}, u32[]{:S(2)}) copy-start(bf16[32,32768]{1,0:T(8,128)(2,1)} %param.8) | copy-start | bytes 6291460
  30.3 19.6 %all-to-all-start.2 = ((bf16[32,16,256]{2,0,1:T(8,128)(2,1)}), bf16[32,16,256]{2,0,1:T(8,128)(2,1)S(1)}, u32[]{:S(2)}, u32[]{:S(2)}) async-start(bf16[32,16,256]{2,0,1:T(8,128)(2,1)} %broadcast_select_fusion), calls=%async_computation.2 | async-start | bytes 524288 | tf_op jit(solution)/shard_map/all_to_all | solution.py:118
  38.4 17.6 %copy-start.4 = (s32[1,1,2048]{2,1,0:T(1,128)S(1)}, s32[1,1,2048]{2,1,0:T(1,128)}, u32[]{:S(2)}) copy-start(s32[1,1,2048]{2,1,0:T(1,128)} %param.15) | copy-start | bytes 24580
  39.9 47.8 %copy-start.5 = (s32[1,1,1024]{2,1,0:T(1,128)S(1)}, s32[1,1,1024]{2,1,0:T(1,128)}, u32[]{:S(2)}) copy-start(s32[1,1,1024]{2,1,0:T(1,128)} %param.14) | copy-start | bytes 12292
  50.0 85.7 %all-to-all-start.1 = ((bf16[16,16,2048]{2,1,0:T(8,128)(2,1)}), bf16[16,16,2048]{2,1,0:T(8,128)(2,1)}, u32[]{:S(2)}, u32[]{:S(2)}) async-start(bf16[16,16,2048]{2,1,0:T(8,128)(2,1)} %get-tuple-element.8), calls=%async_computation.1 | async-start | bytes 2097152 | tf_op jit(solution)/shard_map/all_to_all | solution.py:47
  54.2 27.6 %collective-permute-start.1 = (bf16[1,1,512,256]{3,2,1,0:T(8,128)(2,1)S(1)}, bf16[1,1,512,256]{3,2,1,0:T(8,128)(2,1)S(1)}, u32[]{:S(2)}, u32[]{:S(2)}) collective-permute-start(bf16[1,1,512,256]{3,2,1,0:T(8,128)(2,1)S(1)} %bitcast.116), channel_id=1, source_target_pairs={{16,0},{32,16},{48,32},{64,48},{80,64},{96,80},{112,96},{128,112},... | collective-permute-start | bytes 786440 | tf_op jit(solution)/shard_map/ppermute | solution.py:18
  54.2 27.5 %collective-permute-start = (bf16[1,1,512,256]{3,2,1,0:T(8,128)(2,1)S(1)}, bf16[1,1,512,256]{3,2,1,0:T(8,128)(2,1)S(1)}, u32[]{:S(2)}, u32[]{:S(2)}) collective-permute-start(bf16[1,1,512,256]{3,2,1,0:T(8,128)(2,1)S(1)} %bitcast.117), channel_id=1, source_target_pairs={{0,16},{16,32},{32,48},{48,64},{64,80},{80,96},{96,112},{112,128},... | collective-permute-start | bytes 786440 | tf_op jit(solution)/shard_map/ppermute | solution.py:15
  82.7 32.4 %collective-permute-start.3 = (bf16[1,3,512,256]{3,2,1,0:T(8,128)(2,1)}, bf16[1,3,512,256]{3,2,1,0:T(8,128)(2,1)S(1)}, u32[]{:S(2)}, u32[]{:S(2)}) collective-permute-start(bf16[1,3,512,256]{3,2,1,0:T(8,128)(2,1)} %pad_maximum_fusion.1), channel_id=1, source_target_pairs={{1,0},{2,1},{3,2},{4,3},{5,4},{6,5},{7,6},{8,7},{9,8},{10,9},{11,1... | collective-permute-start | bytes 2359304 | tf_op jit(solution)/shard_map/ppermute | solution.py:18
  87.7 27.5 %collective-permute-start.2 = (bf16[1,3,512,256]{3,2,1,0:T(8,128)(2,1)}, bf16[1,3,512,256]{3,2,1,0:T(8,128)(2,1)}, u32[]{:S(2)}, u32[]{:S(2)}) collective-permute-start(bf16[1,3,512,256]{3,2,1,0:T(8,128)(2,1)} %pad_maximum_fusion.1), channel_id=1, source_target_pairs={{0,1},{1,2},{2,3},{3,4},{4,5},{5,6},{6,7},{7,8},{8,9},{9,10},{10,1... | collective-permute-start | bytes 2359304 | tf_op jit(solution)/shard_map/ppermute | solution.py:15
  87.7 15.4 %collective-permute-start.7 = (bf16[1,3,2,256]{3,2,1,0:T(2,128)(2,1)S(1)}, bf16[1,3,2,256]{3,2,1,0:T(2,128)(2,1)S(1)}, u32[]{:S(2)}, u32[]{:S(2)}) collective-permute-start(bf16[1,3,2,256]{3,2,1,0:T(2,128)(2,1)S(1)} %pad_maximum_fusion.3), channel_id=1, source_target_pairs={{1,0},{2,1},{3,2},{4,3},{5,4},{6,5},{7,6},{8,7},{9,8},{10,9},{11,1... | collective-permute-start | bytes 9224 | tf_op jit(solution)/shard_map/ppermute | solution.py:18
  92.6 15.9 %collective-permute-start.6 = (bf16[1,3,2,256]{3,2,1,0:T(2,128)(2,1)S(1)}, bf16[1,3,2,256]{3,2,1,0:T(2,128)(2,1)S(1)}, u32[]{:S(2)}, u32[]{:S(2)}) collective-permute-start(bf16[1,3,2,256]{3,2,1,0:T(2,128)(2,1)S(1)} %pad_maximum_fusion.3), channel_id=1, source_target_pairs={{0,1},{1,2},{2,3},{3,4},{4,5},{5,6},{6,7},{7,8},{8,9},{9,10},{10,1... | collective-permute-start | bytes 9224 | tf_op jit(solution)/shard_map/ppermute | solution.py:15
  135.2 0.8 copy-start.1
  136.0 36.5 %all-to-all-start = ((bf16[16,16,2048]{2,1,0:T(8,128)(2,1)}), bf16[16,16,2048]{2,1,0:T(8,128)(2,1)S(1)}, u32[]{:S(2)}, u32[]{:S(2)}) async-start(bf16[16,16,2048]{2,1,0:T(8,128)(2,1)} %get-tuple-element.7), calls=%async_computation | async-start | bytes 2097152 | tf_op jit(solution)/shard_map/all_to_all | solution.py:47
  146.8 3.6 %copy-start.2 = (bf16[512,512]{1,0:T(8,128)(2,1)S(1)}, bf16[512,512]{1,0:T(8,128)(2,1)}, u32[]{:S(2)}) copy-start(bf16[512,512]{1,0:T(8,128)(2,1)} %convolution_convert_fusion.3) | copy-start | bytes 1572868
  148.4 0.8 copy-start.3
  155.8 21.7 %collective-permute-start.8 = (bf16[512,512]{1,0:T(8,128)(2,1)S(1)}, bf16[512,512]{1,0:T(8,128)(2,1)S(1)}, u32[]{:S(2)}, u32[]{:S(2)}) collective-permute-start(bf16[512,512]{1,0:T(8,128)(2,1)S(1)} %add_convert_fusion.1), channel_id=1, source_target_pairs={{0,15},{1,0},{2,1},{3,2},{4,3},{5,4},{6,5},{7,6},{8,7},{9,8},{10,9... | collective-permute-start | bytes 1572872 | tf_op jit(solution)/shard_map/ppermute | solution.py:54
where the time goes:
time: 236 us; the launch traced here: 235 us
  waiting for transfers between devices  66.4 us (28%)
  blocking collectives  54.3 us (23%)
  local copies, waits for them, and re-layouts  45.6 us (19%)
  starting transfers between devices  35.8 us (15%)
  matrix products  19.8 us (8%)
  other arithmetic  11.4 us (5%)
    all_to_all x1, blocking collectives, local(): lax.all_to_all(result, 'member', split_axis=0, concat_axis=1, tiled=True)  54.3 us
    ppermute x4, waiting for transfers between devices, with_halo(): lax.ppermute(lax.slice_in_dim(block, 0, width, axis=dim), axis, backward)  34.7 us
    all_to_all x2, waiting for transfers between devices, exchange_in_pieces(): lax.all_to_all(slab, axis, split_axis=0, concat_axis=0, tiled=True)  16.3 us
    gather x2, local copies, waits for them, and re-layouts, local(): mapped_dimension = jnp.take(prior_states, measured_subgrid_line, axis=1)  16 us
    ppermute x4, starting transfers between devices, with_halo(): lax.ppermute(lax.slice_in_dim(block, 0, width, axis=dim), axis, backward)  13 us
    all_to_all x2, starting transfers between devices, exchange_in_pieces(): lax.all_to_all(slab, axis, split_axis=0, concat_axis=0, tiled=True)  12.8 us
    all_to_all x1, waiting for transfers between devices, local(): lax.all_to_all(mapped_dimension, 'member', split_axis=1, concat_axis=0, t...  10.1 us
    unnamed x13, local copies, waits for them, and re-layouts  8.57 us
  transfers between devices with their start and end apart: 12, of which 5 were waited for; matrix products, arithmetic and copies ran while one was open for 30% of the time, Pallas kernels for 0%

commit v1 on v0

v1 whole, which is shorter than its diff:
```python
import functools

import jax
import jax.numpy as jnp
from jax import lax
from jax.experimental import pallas as pl
from jax.experimental.pallas import tpu as pltpu
from jax.sharding import PartitionSpec as P

ITERS = 6
MESH = pl.DeviceIdType.MESH
F32 = jnp.float32
BF16 = jnp.bfloat16
NN = (((1,), (0,)), ((), ()))
NT = (((1,), (1,)), ((), ()))


def dot(a, b, dims=NN):
    return lax.dot_general(a, b, dims, preferred_element_type=F32)


def iota(shape, dim):
    return lax.broadcasted_iota(jnp.int32, shape, dim)


def split_rows(x):
    hi = x.astype(BF16).astype(F32)
    mid = (x - hi).astype(BF16).astype(F32)
    low = x - hi - mid
    row = iota((16, x.shape[1]), 0)
    rows = jnp.where(row == 0, hi, jnp.where(row == 1, mid, jnp.where(row == 2, low, 0.0)))
    return rows.astype(BF16)


def row_dot(x, b, dims):
    return jnp.sum(dot(split_rows(x), b, dims), axis=0, keepdims=True)


def kernel(
    n, regions,
    prior, line, data, lookup, dist, share, count,
    out,
    pv, state, psend, blocks, pert, wp, want, asked, gs, gr, vs, vr, amat, y, z, t, ye, fs, fe, res,
    load_sem, in_s, in_r, pr_s, pr_r, halo_s, halo_r, want_s, want_r, g_s, g_r, v_s, v_r, y_s, y_r, f_s, f_r, out_s, out_r,
):
    p = lax.axis_index("member")
    s = lax.axis_index("region")
    members = 512 // n
    west, east = lax.rem(s + regions - 1, regions), lax.rem(s + 1, regions)

    def remote(src, dst, ss, rs, **where):
        return pltpu.make_async_remote_copy(
            src_ref=src, dst_ref=dst, send_sem=ss, recv_sem=rs, device_id=where, device_id_type=MESH
        )

    def peer(d):
        return lax.rem(p + d, n)

    def my_rows(ref, k):
        return ref.at[pl.ds(pl.multiple_of(k * members, members), members)]

    def band(ref, k):
        return ref.at[:, pl.ds(pl.multiple_of(k * 2048, 2048), 2048)]

    load = pltpu.make_async_copy(prior, pv, load_sem)
    load.start()
    barrier = pltpu.get_barrier_semaphore()

    def greet(d, carry):
        pl.semaphore_signal(barrier, inc=1, device_id={"member": peer(d)}, device_id_type=MESH)
        return carry

    lax.fori_loop(1, n, greet, 0)
    for other in (west, east):
        pl.semaphore_signal(barrier, inc=1, device_id={"region": other}, device_id_type=MESH)

    slots = lookup.shape[-1]
    named = lookup[0, pl.ds(p, 1), :]
    side = lax.shift_right_logical(named, 12)
    offset = (lax.shift_right_logical(named, 8) & 15) - p + 1
    live = iota((1, slots), 1) < count[0, 0]
    code = jnp.where(live, (dist[0] + 1).astype(F32), 0.0)
    group = jnp.where(iota((32, slots), 0) == side * 8 + offset, code, 0.0).astype(BF16)
    place = jnp.where(iota((256, slots), 0) == (named & 255), 1.0, 0.0).astype(BF16)
    want[...] = dot(group, place, NT)

    load.wait()
    pl.semaphore_wait(barrier, n + 1)

    def state_copy(d):
        q = peer(d)
        return remote(band(pv, q), my_rows(state, p), in_s.at[d], in_r.at[d], member=q)

    def send_state(pairs):
        for k in pairs:
            state_copy(k).start()
            if 2 * k != n:
                state_copy(n - k).start()

    send_state((1, 2))
    want_west = remote(want.at[pl.ds(0, 8)], asked.at[1], want_s.at[0], want_r.at[1], region=west)
    want_east = remote(want.at[pl.ds(16, 8)], asked.at[0], want_s.at[1], want_r.at[0], region=east)
    want_west.start()
    want_east.start()

    def project(q):
        rows = [pv[:, pl.ds(pl.multiple_of(q * 2048 + 256 * h, 256), 256)] for h in range(8)]
        at = line[pl.ds(q, 1), :]
        pick = jnp.where(iota((256, 256), 0) == (at & 255), 1.0, 0.0).astype(BF16)
        found = dot(jnp.concatenate(rows, axis=0), pick)
        high = lax.shift_right_logical(at, 8) & 7
        total = jnp.zeros((members, 256), F32)
        for h in range(8):
            total = total + jnp.where(high == h, found[members * h : members * (h + 1)], 0.0)
        return total.astype(BF16)

    def proj_copy(d):
        q = peer(d)
        return remote(psend.at[q], my_rows(blocks.at[1], p), pr_s.at[d], pr_r.at[d], member=q)

    def project_one(d, carry):
        q = peer(d)
        psend[q] = project(q)
        proj_copy(d).start()
        return carry

    lax.fori_loop(1, n, project_one, 0)
    send_state((3, 4))
    blocks[1, pl.ds(pl.multiple_of(p * members, members), members), :] = project(p)
    own = pltpu.make_async_copy(band(pv, p), my_rows(state, p), load_sem)
    own.start()

    def proj_wait(d, carry):
        proj_copy(d).wait_recv()
        return carry

    lax.fori_loop(1, n, proj_wait, 0)
    up = remote(blocks.at[1], blocks.at[0], halo_s.at[0], halo_r.at[0], member=peer(1))
    down = remote(blocks.at[1], blocks.at[2], halo_s.at[1], halo_r.at[1], member=peer(n - 1))
    up.start()
    down.start()
    send_state((5, 6, 7, 8))

    departs, precision = [None] * 3, [None] * 3

    def centre(j):
        values = blocks[j].astype(F32)
        ybar = jnp.mean(values, axis=0, keepdims=True)
        pert[:, 256 * j : 256 * (j + 1)] = (values - ybar).astype(BF16)
        k = lax.rem(p + n - 1 + j, n)
        departs[j] = data[0, pl.ds(k, 1), :] - ybar
        precision[j] = data[1, pl.ds(k, 1), :]

    centre(1)
    up.wait_recv()
    centre(0)
    down.wait_recv()
    centre(2)
    want_west.wait_recv()
    want_east.wait_recv()

    def weigh(asks):
        moments = []
        for j in range(3):
            code = asks[j : j + 1, :]
            w = jnp.where(code > 0.0, precision[j] * 2.0 / (1.0 + code), 0.0)
            cols = slice(256 * j, 256 * (j + 1))
            wp[:, cols] = (pert[:, cols].astype(F32) * w).astype(BF16)
            moments.append(w * departs[j])
        return row_dot(jnp.concatenate(moments, axis=1), pert[...], NT)

    def gram(i):
        return dot(wp[128 * i : 128 * (i + 1), :], pert[128 * i :, :], NT)

    def gram_copy(side, i, where):
        part = (pl.ds(128 * i, 128), pl.ds(128 * i, 512 - 128 * i))
        return remote(gs.at[side].at[part], gr.at[1 - side].at[part], g_s.at[side, i], g_r.at[1 - side, i], region=where)

    def moment_copy(side, where):
        return remote(vs.at[side], vr.at[1 - side], v_s.at[side], v_r.at[1 - side], region=where)

    for side_, where in ((0, west), (1, east)):
        moment = weigh(asked[side_])
        vs[side_] = jnp.broadcast_to(moment, (8, 512))
        moment_copy(side_, where).start()
        for i in range(4):
            gs[side_, 128 * i : 128 * (i + 1), 128 * i :] = gram(i).astype(BF16)
            gram_copy(side_, i, where).start()
    gvec = weigh(want[8:16, :])
    for i in range(4):
        amat[128 * i : 128 * (i + 1), 128 * i :] = gram(i)

    def eye(rows, cols, at):
        return iota((rows, cols), 0) + at == iota((rows, cols), 1)

    squares = jnp.zeros((1, 1), F32)
    for i in range(4):
        for side_, where in ((0, west), (1, east)):
            gram_copy(side_, i, where).wait_recv()
        rows, width = slice(128 * i, 128 * (i + 1)), 512 - 128 * i
        a = amat[rows, 128 * i :] + (gr[0, rows, 128 * i :].astype(F32) + gr[1, rows, 128 * i :].astype(F32))
        a = a + jnp.where(eye(128, width, 0), 511.0, 0.0)
        amat[rows, 128 * i :] = a
        twice = a * a * jnp.where(iota((1, width), 1) < 128, 1.0, 2.0)
        squares = squares + jnp.sum(jnp.sum(twice, axis=0, keepdims=True), axis=1, keepdims=True)
    norm = jnp.sqrt(squares)
    inverse = 1.0 / norm
    for i in range(4):
        rows = slice(128 * i, 128 * (i + 1))
        scaled = amat[rows, 128 * i :] * inverse
        z[0, rows, 128 * i :] = scaled.astype(BF16)
        for j in range(i + 1, 4):
            z[0, 128 * j : 128 * (j + 1), rows] = scaled[:, 128 * (j - i) : 128 * (j - i + 1)].T.astype(BF16)

    half = 256
    halves = [slice(0, half), slice(half, 512)]
    for k, rows in enumerate(halves):
        first = jnp.where(eye(half, 512, half * k), 1.5, 0.0) - 0.5 * z[0, rows, :].astype(F32)
        y[1, rows, :] = first.astype(BF16)
    for rows in halves:
        z[1, rows, :] = dot(y[1, rows, :], z[0]).astype(BF16)

    def make_t(now):
        for k, rows in enumerate(halves):
            product = dot(z[now, rows, :], y[now])
            t[rows, :] = (jnp.where(eye(half, 512, half * k), 1.5, 0.0) - 0.5 * product).astype(BF16)

    def step(it, carry):
        now = lax.rem(it, 2)
        make_t(now)
        for rows in halves:
            y[1 - now, rows, :] = dot(y[now, rows, :], t[...]).astype(BF16)
            z[1 - now, rows, :] = dot(t[rows, :], z[now]).astype(BF16)
        return carry

    lax.fori_loop(1, ITERS - 1, step, 0)
    last = (ITERS - 1) % 2
    make_t(last)
    yf = y.at[1 - last]
    for rows in halves:
        yf[rows, :] = dot(y[last, rows, :], t[...]).astype(BF16)

    def east_copy(d):
        q = peer(d)
        return remote(my_rows(yf, q), my_rows(ye, q), y_s.at[d], y_r.at[d], region=west)

    def east_send(d, carry):
        east_copy(d).start()
        return carry

    lax.fori_loop(0, n, east_send, 0)
    for side_, where in ((0, west), (1, east)):
        moment_copy(side_, where).wait_recv()
    gvec = gvec + (vr[0, 0:1, :] + vr[1, 0:1, :])
    root = jnp.sqrt(norm)
    wbar = row_dot(row_dot(gvec, yf[...], NT) / root, yf[...], NT) / root
    scale = jnp.sqrt(F32(511.0)) / root
    fs[...] = jnp.where(iota((8, 512), 0) == 0, wbar, jnp.broadcast_to(scale, (8, 512)))
    factors = remote(fs, fe, f_s, f_r, region=west)
    factors.start()

    own.wait()

    def state_wait(d, carry):
        state_copy(d).wait_recv()
        return carry

    lax.fori_loop(1, n, state_wait, 0)
    xbars, bases, owns, easts = [], [], [], []
    tile = 512
    for c in range(4):
        cols = slice(tile * c, tile * (c + 1))
        values = state[:, cols].astype(F32)
        xbar = jnp.mean(values, axis=0, keepdims=True)
        state[:, cols] = (values - xbar).astype(BF16)
        xbars.append(xbar)
    factors.wait_recv()
    for c in range(4):
        cols = slice(tile * c, tile * (c + 1))
        part = share[0, :, cols].astype(F32) * 0.125
        shift_own = row_dot(wbar, state[:, cols], NN)
        shift_east = row_dot(fe[0:1, :], state[:, cols], NN)
        bases.append(xbars[c] + (1.0 - part) * shift_own + part * shift_east)
        owns.append((1.0 - part) * scale)
        easts.append(part * fe[1:2, 0:tile])

    def out_copy(d):
        q = peer(d)
        return remote(res.at[q], band(out, p), out_s.at[d], out_r.at[d], member=q)

    def update(q):
        at = pl.ds(pl.multiple_of(q * members, members), members)
        lhs = jnp.concatenate([yf[at, :], ye[at, :]], axis=0)
        for c in range(4):
            cols = slice(tile * c, tile * (c + 1))
            both = dot(lhs, state[:, cols])
            value = bases[c] + owns[c] * both[:members] + easts[c] * both[members:]
            res[q, :, cols] = value.astype(BF16)

    def update_one(d, carry):
        east_copy(d).wait_recv()
        update(peer(d))
        out_copy(d).start()
        return carry

    lax.fori_loop(1, n, update_one, 0)
    east_copy(0).wait_recv()
    update(p)
    mine = pltpu.make_async_copy(res.at[p], band(out, p), load_sem)
    mine.start()

    def finish(d, carry):
        out_copy(d).wait()
        state_copy(d).wait_send()
        proj_copy(d).wait_send()
        east_copy(d).wait_send()
        return carry

    lax.fori_loop(1, n, finish, 0)
    east_copy(0).wait_send()
    mine.wait()
    for c in (want_west, want_east, up, down, factors):
        c.wait_send()
    for side_, where in ((0, west), (1, east)):
        moment_copy(side_, where).wait_send()
        for i in range(4):
            gram_copy(side_, i, where).wait_send()


def local(n, regions, prior, values, precision, line, lookup, count, dist, share):
    data = jnp.stack((values, precision)).astype(F32).reshape(2, n, -1)
    dma = pltpu.SemaphoreType.DMA
    vmem = pl.BlockSpec(memory_space=pltpu.VMEM)
    members = prior.shape[0]
    return pl.pallas_call(
        functools.partial(kernel, n, regions),
        out_shape=jax.ShapeDtypeStruct(prior.shape, BF16),
        in_specs=[pl.BlockSpec(memory_space=pl.ANY)] + [vmem] * 5 + [pl.BlockSpec(memory_space=pltpu.SMEM)],
        out_specs=pl.BlockSpec(memory_space=pl.ANY),
        scratch_shapes=[
            pltpu.VMEM(prior.shape, BF16),
            pltpu.VMEM((512, 2048), BF16),
            pltpu.VMEM((n, members, 256), BF16),
            pltpu.VMEM((3, 512, 256), BF16),
            pltpu.VMEM((512, 768), BF16),
            pltpu.VMEM((512, 768), BF16),
            pltpu.VMEM((32, 256), F32),
            pltpu.VMEM((2, 8, 256), F32),
            pltpu.VMEM((2, 512, 512), BF16),
            pltpu.VMEM((2, 512, 512), BF16),
            pltpu.VMEM((2, 8, 512), F32),
            pltpu.VMEM((2, 8, 512), F32),
            pltpu.VMEM((512, 512), F32),
            pltpu.VMEM((2, 512, 512), BF16),
            pltpu.VMEM((2, 512, 512), BF16),
            pltpu.VMEM((512, 512), BF16),
            pltpu.VMEM((512, 512), BF16),
            pltpu.VMEM((8, 512), F32),
            pltpu.VMEM((8, 512), F32),
            pltpu.VMEM((n, members, 2048), BF16),
            dma,
            dma((n,)), dma((n,)),
            dma((n,)), dma((n,)),
            dma((2,)), dma((2,)),
            dma((2,)), dma((2,)),
            dma((2, 4)), dma((2, 4)),
            dma((2,)), dma((2,)),
            dma((n,)), dma((n,)),
            dma, dma,
            dma((n,)), dma((n,)),
        ],
        compiler_params=pltpu.CompilerParams(
            collective_id=0, has_side_effects=True, vmem_limit_bytes=40 * 1024 * 1024
        ),
    )(prior, line.reshape(n, -1), data, lookup, dist, share, count)


def solution(mesh):
    in_specs = (
        P("member", "region"),
        P("region"),
        P("region"),
        P("region"),
        P("region", None, None),
        P("region", "member"),
        P("region", "member", None),
        P("region", "member", None),
    )
    body = functools.partial(local, mesh.shape["member"], mesh.shape["region"])
    return jax.shard_map(body, mesh=mesh, in_specs=in_specs, out_specs=P("member", "region"), check_vma=False)
```

time: 236 us -> 136 us (0.58)
  Pallas kernels: 0 us -> 125 us
  waiting for transfers between devices: 66.4 us -> 0 us
  blocking collectives: 54.3 us -> 0 us
  local copies, waits for them, and re-layouts: 45.6 us -> 7.27 us
  starting transfers between devices: 35.8 us -> 0 us
  matrix products: 19.8 us -> 0 us
  other arithmetic: 11.4 us -> 0.01 us
    pallas_call x0 -> x1, Pallas kernels: none -> 125 us  [local(): pl.pallas_call(functools.partial(kernel, n, regions), out_shape=jax.Shape...]
    all_to_all x1 -> x0, blocking collectives: 54.3 us -> none  [local(): lax.all_to_all(result, 'member', split_axis=0, concat_axis=1, tiled=True)]
    ppermute x9 -> x0, waiting for transfers between devices: 40 us -> none  [the longest x4 34.7 us: with_halo(): lax.ppermute(lax.slice_in_dim(block, 0, width, axis=dim), axis, backward)]
    gather x4 -> x0, local copies, waits for them, and re-layouts: 29.1 us -> none  [the longest x2 16 us: local(): mapped_dimension = jnp.take(prior_states, measured_subgrid_line, axis=1)]
    all_to_all x3 -> x0, waiting for transfers between devices: 26.4 us -> none  [the longest x2 16.3 us: exchange_in_pieces(): lax.all_to_all(slab, axis, split_axis=0, concat_axis=0, tiled=True)]
    all_to_all x3 -> x0, starting transfers between devices: 20.7 us -> none  [the longest x2 12.8 us: exchange_in_pieces(): lax.all_to_all(slab, axis, split_axis=0, concat_axis=0, tiled=True)]
    dot_general x21 -> x0, matrix products: 19.8 us -> none  [the longest x6 5.98 us: transform(): product = jnp.dot(zmat, ymat, preferred_element_type=jnp.float32)]
    ppermute x9 -> x0, starting transfers between devices: 15.1 us -> none  [the longest x4 13 us: with_halo(): lax.ppermute(lax.slice_in_dim(block, 0, width, axis=dim), axis, backward)]
  transfers between devices with their start and end apart: 12 -> 0, of which waited for: 5 -> 0; matrix products, arithmetic and copies ran while one was open for 30% -> 0% of each run, Pallas kernels for 0% -> 0%
where the time goes in v1:
time: 136 us; the launch traced here: 133 us
  Pallas kernels  125 us (92%)
  local copies, waits for them, and re-layouts  7.27 us (5%)
    pallas_call x1, Pallas kernels, local(): pl.pallas_call(functools.partial(kernel, n, regions), out_shape=jax.Shape...  125 us
    unnamed x9, local copies, waits for them, and re-layouts  5.13 us

profile of v1, /device:TPU:1, one launch (start us, length us, event | category | flops | bytes accessed | tf_op | source)
XLA Modules:
  0.0 133.1 jit_solution(10416794162954700991)
XLA Ops:
  0.7 0.7 stack.9
  1.4 0.7 stack.10
  2.1 0.7 reshape.8.line
  2.8 0.0 copy-start
  2.8 1.6 %copy-done = bf16[32,32768]{1,0:T(8,128)(2,1)S(1)} copy-done((bf16[32,32768]{1,0:T(8,128)(2,1)S(1)}, bf16[32,32768]{1,0:T(8,128)(2,1)}, u32[]{:S(2)}) %copy-start) | copy-done | bytes 2097176
  4.4 0.0 copy-start.1
  4.4 0.8 copy-done.1
  5.2 0.0 copy-start.2
  5.2 0.7 copy-done.2
  5.9 0.0 copy-start.3
  5.9 0.7 copy-done.3
  6.6 125.1 %shard_map.82 = bf16[32,32768]{1,0:T(8,128)(2,1)S(1)} custom-call(bf16[32,32768]{1,0:T(8,128)(2,1)S(1)} %copy-done, s32[16,256]{1,0:T(8,128)S(1)} %reshape.8.line, f32[2,16,256]{2,1,0:T(8,128)S(1)} %maximum_convert_fusion.data, s32[1,16,1024]{2,1,0:T(8,128)S(1)} %copy-done.1, s32[1,1,1024]{2,1,0:T(1,128)S(1)} %copy-done.3, s32[1,1,2048]{2,1,0:T(1,128)S(1)} %copy-done.2, ...), custom_call_target="tpu_custom_call" | custom-call | tf_op jit(solution)/shard_map/pallas_call | solution.py:335
  131.7 1.3 copy.11
  (1 shorter events, 0.0 us)
Async XLA Ops:
  2.8 1.6 %copy-start = (bf16[32,32768]{1,0:T(8,128)(2,1)S(1)}, bf16[32,32768]{1,0:T(8,128)(2,1)}, u32[]{:S(2)}) copy-start(bf16[32,32768]{1,0:T(8,128)(2,1)} %prior.1) | copy-start | bytes 6291460
  4.4 0.8 copy-start.1
  5.2 0.7 copy-start.2
  5.9 0.7 copy-start.3

commit v2 on v1

--- a/solution.py
+++ b/solution.py
@@ -38,10 +38,10 @@
 
 def kernel(
     n, regions,
-    prior, line, data, lookup, dist, share, count,
+    prior, line_in, values_in, precision_in, lookup_in, dist_in, share_in, count,
     out,
-    pv, state, psend, blocks, pert, wp, want, asked, gs, gr, vs, vr, amat, y, z, t, ye, fs, fe, res,
-    load_sem, in_s, in_r, pr_s, pr_r, halo_s, halo_r, want_s, want_r, g_s, g_r, v_s, v_r, y_s, y_r, f_s, f_r, out_s, out_r,
+    line, values, precisions, data, lookup, dist, share, pv, state, psend, blocks, pert, wp, want, asked, gs, gr, vs, vr, amat, y, z, t, ye, fs, fe, res,
+    load_sem, small_sem, in_s, in_r, pr_s, pr_r, halo_s, halo_r, want_s, want_r, g_s, g_r, v_s, v_r, y_s, y_r, f_s, f_r, out_s, out_r,
 ):
     p = lax.axis_index("member")
     s = lax.axis_index("region")
@@ -64,6 +64,21 @@
 
     load = pltpu.make_async_copy(prior, pv, load_sem)
     load.start()
+    smalls = [
+        pltpu.make_async_copy(src, dst, small_sem.at[k])
+        for k, (src, dst) in enumerate(
+            (
+                (lookup_in, lookup),
+                (dist_in, dist),
+                (line_in, line),
+                (values_in, values),
+                (precision_in, precisions),
+                (share_in, share),
+            )
+        )
+    ]
+    for c in smalls:
+        c.start()
     barrier = pltpu.get_barrier_semaphore()
 
     def greet(d, carry):
@@ -73,6 +88,14 @@
     lax.fori_loop(1, n, greet, 0)
     for other in (west, east):
         pl.semaphore_signal(barrier, inc=1, device_id={"region": other}, device_id_type=MESH)
+
+    def pair(ref, k):
+        return jnp.concatenate([ref[pl.ds(2 * k, 1), :], ref[pl.ds(2 * k + 1, 1), :]], axis=1)
+
+    for c in smalls:
+        c.wait()
+    data[0:32, :] = values[...].astype(F32)
+    data[32:64, :] = precisions[...].astype(F32)
 
     slots = lookup.shape[-1]
     named = lookup[0, pl.ds(p, 1), :]
@@ -84,28 +107,9 @@
     place = jnp.where(iota((256, slots), 0) == (named & 255), 1.0, 0.0).astype(BF16)
     want[...] = dot(group, place, NT)
 
-    load.wait()
-    pl.semaphore_wait(barrier, n + 1)
-
-    def state_copy(d):
-        q = peer(d)
-        return remote(band(pv, q), my_rows(state, p), in_s.at[d], in_r.at[d], member=q)
-
-    def send_state(pairs):
-        for k in pairs:
-            state_copy(k).start()
-            if 2 * k != n:
-                state_copy(n - k).start()
-
-    send_state((1, 2))
-    want_west = remote(want.at[pl.ds(0, 8)], asked.at[1], want_s.at[0], want_r.at[1], region=west)
-    want_east = remote(want.at[pl.ds(16, 8)], asked.at[0], want_s.at[1], want_r.at[0], region=east)
-    want_west.start()
-    want_east.start()
-
     def project(q):
         rows = [pv[:, pl.ds(pl.multiple_of(q * 2048 + 256 * h, 256), 256)] for h in range(8)]
-        at = line[pl.ds(q, 1), :]
+        at = pair(line, q)
         pick = jnp.where(iota((256, 256), 0) == (at & 255), 1.0, 0.0).astype(BF16)
         found = dot(jnp.concatenate(rows, axis=0), pick)
         high = lax.shift_right_logical(at, 8) & 7
@@ -114,19 +118,41 @@
             total = total + jnp.where(high == h, found[members * h : members * (h + 1)], 0.0)
         return total.astype(BF16)
 
+    load.wait()
+
+    def project_one(q, carry):
+        psend[q] = project(q)
+        return carry
+
+    lax.fori_loop(0, n, project_one, 0)
+    pl.semaphore_wait(barrier, n + 1)
+
+    def state_copy(d):
+        q = peer(d)
+        return remote(band(pv, q), my_rows(state, p), in_s.at[d], in_r.at[d], member=q)
+
+    def send_state(pairs):
+        for k in pairs:
+            state_copy(k).start()
+            if 2 * k != n:
+                state_copy(n - k).start()
+
+    want_west = remote(want.at[pl.ds(0, 8)], asked.at[1], want_s.at[0], want_r.at[1], region=west)
+    want_east = remote(want.at[pl.ds(16, 8)], asked.at[0], want_s.at[1], want_r.at[0], region=east)
+
     def proj_copy(d):
         q = peer(d)
         return remote(psend.at[q], my_rows(blocks.at[1], p), pr_s.at[d], pr_r.at[d], member=q)
 
-    def project_one(d, carry):
-        q = peer(d)
-        psend[q] = project(q)
+    def proj_send(d, carry):
         proj_copy(d).start()
         return carry
 
-    lax.fori_loop(1, n, project_one, 0)
-    send_state((3, 4))
-    blocks[1, pl.ds(pl.multiple_of(p * members, members), members), :] = project(p)
+    lax.fori_loop(1, n, proj_send, 0)
+    want_west.start()
+    want_east.start()
+    send_state((1, 2))
+    blocks[1, pl.ds(pl.multiple_of(p * members, members), members), :] = psend[p]
     own = pltpu.make_async_copy(band(pv, p), my_rows(state, p), load_sem)
     own.start()
 
@@ -139,7 +165,7 @@
     down = remote(blocks.at[1], blocks.at[2], halo_s.at[1], halo_r.at[1], member=peer(n - 1))
     up.start()
     down.start()
-    send_state((5, 6, 7, 8))
+    send_state((3, 4, 5, 6, 7, 8))
 
     departs, precision = [None] * 3, [None] * 3
 
@@ -148,8 +174,8 @@
         ybar = jnp.mean(values, axis=0, keepdims=True)
         pert[:, 256 * j : 256 * (j + 1)] = (values - ybar).astype(BF16)
         k = lax.rem(p + n - 1 + j, n)
-        departs[j] = data[0, pl.ds(k, 1), :] - ybar
-        precision[j] = data[1, pl.ds(k, 1), :]
+        departs[j] = pair(data, k) - ybar
+        precision[j] = pair(data, n + k)
 
     centre(1)
     up.wait_recv()
@@ -266,21 +292,23 @@
         return carry
 
     lax.fori_loop(1, n, state_wait, 0)
-    xbars, bases, owns, easts = [], [], [], []
+    factors.wait_recv()
+    sums, bases, owns, easts = [], [], [], []
     tile = 512
-    for c in range(4):
-        cols = slice(tile * c, tile * (c + 1))
-        values = state[:, cols].astype(F32)
-        xbar = jnp.mean(values, axis=0, keepdims=True)
-        state[:, cols] = (values - xbar).astype(BF16)
-        xbars.append(xbar)
-    factors.wait_recv()
+    wide = jnp.concatenate(
+        [split_rows(wbar), split_rows(fe[0:1, :]), jnp.ones((16, 512), BF16)], axis=0
+    )
+    totals = [jnp.sum(w, axis=1, keepdims=True) for w in (wbar, fe[0:1, :])]
     for c in range(4):
         cols = slice(tile * c, tile * (c + 1))
         part = share[0, :, cols].astype(F32) * 0.125
-        shift_own = row_dot(wbar, state[:, cols], NN)
-        shift_east = row_dot(fe[0:1, :], state[:, cols], NN)
-        bases.append(xbars[c] + (1.0 - part) * shift_own + part * shift_east)
+        rows = dot(wide, state[:, cols])
+        xbar = rows[32:33] * (1.0 / 512.0)
+        shifts = [
+            jnp.sum(rows[16 * k : 16 * (k + 1)], axis=0, keepdims=True) - totals[k] * xbar for k in range(2)
+        ]
+        sums.append(xbar)
+        bases.append(xbar + (1.0 - part) * shifts[0] + part * shifts[1])
         owns.append((1.0 - part) * scale)
         easts.append(part * fe[1:2, 0:tile])
 
@@ -291,9 +319,10 @@
     def update(q):
         at = pl.ds(pl.multiple_of(q * members, members), members)
         lhs = jnp.concatenate([yf[at, :], ye[at, :]], axis=0)
+        weight = jnp.sum(lhs.astype(F32), axis=1, keepdims=True)
         for c in range(4):
             cols = slice(tile * c, tile * (c + 1))
-            both = dot(lhs, state[:, cols])
+            both = dot(lhs, state[:, cols]) - weight * sums[c]
             value = bases[c] + owns[c] * both[:members] + easts[c] * both[members:]
             res[q, :, cols] = value.astype(BF16)
 
@@ -328,16 +357,22 @@
 
 
 def local(n, regions, prior, values, precision, line, lookup, count, dist, share):
-    data = jnp.stack((values, precision)).astype(F32).reshape(2, n, -1)
     dma = pltpu.SemaphoreType.DMA
-    vmem = pl.BlockSpec(memory_space=pltpu.VMEM)
+    hbm = pl.BlockSpec(memory_space=pltpu.HBM)
     members = prior.shape[0]
     return pl.pallas_call(
         functools.partial(kernel, n, regions),
         out_shape=jax.ShapeDtypeStruct(prior.shape, BF16),
-        in_specs=[pl.BlockSpec(memory_space=pl.ANY)] + [vmem] * 5 + [pl.BlockSpec(memory_space=pltpu.SMEM)],
+        in_specs=[hbm] * 7 + [pl.BlockSpec(memory_space=pltpu.SMEM)],
         out_specs=pl.BlockSpec(memory_space=pl.ANY),
         scratch_shapes=[
+            pltpu.VMEM((32, 128), jnp.int32),
+            pltpu.VMEM((32, 128), BF16),
+            pltpu.VMEM((32, 128), BF16),
+            pltpu.VMEM((64, 128), F32),
+            pltpu.VMEM(lookup.shape, jnp.int32),
+            pltpu.VMEM(dist.shape, jnp.int32),
+            pltpu.VMEM(share.shape, jnp.int32),
             pltpu.VMEM(prior.shape, BF16),
             pltpu.VMEM((512, 2048), BF16),
             pltpu.VMEM((n, members, 256), BF16),
@@ -358,7 +393,7 @@
             pltpu.VMEM((8, 512), F32),
             pltpu.VMEM((8, 512), F32),
             pltpu.VMEM((n, members, 2048), BF16),
-            dma,
+            dma, dma((6,)),
             dma((n,)), dma((n,)),
             dma((n,)), dma((n,)),
             dma((2,)), dma((2,)),
@@ -370,9 +405,9 @@
             dma((n,)), dma((n,)),
         ],
         compiler_params=pltpu.CompilerParams(
-            collective_id=0, has_side_effects=True, vmem_limit_bytes=40 * 1024 * 1024
+            collective_id=0, has_side_effects=True, vmem_limit_bytes=63 * 1024 * 1024
         ),
-    )(prior, line.reshape(n, -1), data, lookup, dist, share, count)
+    )(prior, *(a.reshape(-1, 128) for a in (line, values, precision)), lookup, dist, share, count)
 
 
 def solution(mesh):

time: 136 us -> 120 us (0.88); the launches traced: 133 us -> 119 us
  Pallas kernels: 125 us -> 116 us
  local copies, waits for them, and re-layouts: 7.27 us -> 3.05 us
    pallas_call x1, Pallas kernels: 125 us -> 116 us  [local(): pl.pallas_call(functools.partial(kernel, n, regions), out_shape=jax.Shape...]
    unnamed x9 -> x1, local copies, waits for them, and re-layouts: 5.13 us -> 3.05 us
    another operation x2 -> x0, local copies, waits for them, and re-layouts: 1.41 us -> none  [local(): data = jnp.stack((values, precision)).astype(F32).reshape(2, n, -1)]
where the time goes in v2:
time: 120 us; the launch traced here: 119 us
  Pallas kernels  116 us (97%)
  local copies, waits for them, and re-layouts  3.05 us (3%)
    pallas_call x1, Pallas kernels, local(): pl.pallas_call(functools.partial(kernel, n, regions), out_shape=jax.Shape...  116 us
    unnamed x1, local copies, waits for them, and re-layouts  3.05 us

profile of v2, /device:TPU:1, one launch (start us, length us, event | category | flops | bytes accessed | tf_op | source)
XLA Modules:
  0.0 119.4 jit_solution(4735865658840723436)
XLA Ops:
  0.7 115.7 %shard_map.82 = bf16[32,32768]{1,0:T(8,128)(2,1)} custom-call(bf16[32,32768]{1,0:T(8,128)(2,1)} %prior.1, s32[32,128]{1,0:T(8,128)} %bitcast.3, bf16[32,128]{1,0:T(8,128)(2,1)} %bitcast.4, bf16[32,128]{1,0:T(8,128)(2,1)} %bitcast.5, s32[1,16,1024]{2,1,0:T(8,128)} %lookup_in.1, s32[1,1,1024]{2,1,0:T(1,128)} %dist_in.1, s32[1,1,2048]{2,1,0:T(1,128)} %share_in.1, ...), custom_call_target="tpu_custom_call" | custom-call | tf_op jit(solution)/shard_map/pallas_call | solution.py:363
  116.3 3.0 %copy.11 = bf16[32,32768]{1,0:T(8,128)(2,1)} copy(bf16[32,32768]{1,0:T(8,128)(2,1)} %shard_map.82) | data formatting | bytes 4194304

commit v3 on v2

--- a/solution.py
+++ b/solution.py
@@ -41,7 +41,7 @@
     prior, line_in, values_in, precision_in, lookup_in, dist_in, share_in, count,
     out,
     line, values, precisions, data, lookup, dist, share, pv, state, psend, blocks, pert, wp, want, asked, gs, gr, vs, vr, amat, y, z, t, ye, fs, fe, res,
-    load_sem, small_sem, in_s, in_r, pr_s, pr_r, halo_s, halo_r, want_s, want_r, g_s, g_r, v_s, v_r, y_s, y_r, f_s, f_r, out_s, out_r,
+    load_sem, small_sem, own_sem, in_s, in_r, pr_s, pr_r, halo_s, halo_r, want_s, want_r, g_s, g_r, v_s, v_r, y_s, y_r, f_s, f_r, out_s, out_r,
 ):
     p = lax.axis_index("member")
     s = lax.axis_index("region")
@@ -56,11 +56,25 @@
     def peer(d):
         return lax.rem(p + d, n)
 
+    def nth(i):
+        k = n // 2 - lax.div(i + 1, 2)
+        return jnp.where(lax.rem(i, 2) == 1, k, n - k)
+
     def my_rows(ref, k):
         return ref.at[pl.ds(pl.multiple_of(k * members, members), members)]
 
-    def band(ref, k):
-        return ref.at[:, pl.ds(pl.multiple_of(k * 2048, 2048), 2048)]
+    def half_band(ref, k, h):
+        return ref.at[:, pl.ds(pl.multiple_of(k * 2048 + 1024 * h, 1024), 1024)]
+
+    barrier = pltpu.get_barrier_semaphore()
+
+    def greet(d, carry):
+        pl.semaphore_signal(barrier, inc=1, device_id={"member": peer(d)}, device_id_type=MESH)
+        return carry
+
+    lax.fori_loop(1, n, greet, 0)
+    for other in (west, east):
+        pl.semaphore_signal(barrier, inc=1, device_id={"region": other}, device_id_type=MESH)
 
     load = pltpu.make_async_copy(prior, pv, load_sem)
     load.start()
@@ -68,9 +82,9 @@
         pltpu.make_async_copy(src, dst, small_sem.at[k])
         for k, (src, dst) in enumerate(
             (
+                (line_in, line),
                 (lookup_in, lookup),
                 (dist_in, dist),
-                (line_in, line),
                 (values_in, values),
                 (precision_in, precisions),
                 (share_in, share),
@@ -79,33 +93,8 @@
     ]
     for c in smalls:
         c.start()
-    barrier = pltpu.get_barrier_semaphore()
-
-    def greet(d, carry):
-        pl.semaphore_signal(barrier, inc=1, device_id={"member": peer(d)}, device_id_type=MESH)
-        return carry
-
-    lax.fori_loop(1, n, greet, 0)
-    for other in (west, east):
-        pl.semaphore_signal(barrier, inc=1, device_id={"region": other}, device_id_type=MESH)
-
     def pair(ref, k):
         return jnp.concatenate([ref[pl.ds(2 * k, 1), :], ref[pl.ds(2 * k + 1, 1), :]], axis=1)
-
-    for c in smalls:
-        c.wait()
-    data[0:32, :] = values[...].astype(F32)
-    data[32:64, :] = precisions[...].astype(F32)
-
-    slots = lookup.shape[-1]
-    named = lookup[0, pl.ds(p, 1), :]
-    side = lax.shift_right_logical(named, 12)
-    offset = (lax.shift_right_logical(named, 8) & 15) - p + 1
-    live = iota((1, slots), 1) < count[0, 0]
-    code = jnp.where(live, (dist[0] + 1).astype(F32), 0.0)
-    group = jnp.where(iota((32, slots), 0) == side * 8 + offset, code, 0.0).astype(BF16)
-    place = jnp.where(iota((256, slots), 0) == (named & 255), 1.0, 0.0).astype(BF16)
-    want[...] = dot(group, place, NT)
 
     def project(q):
         rows = [pv[:, pl.ds(pl.multiple_of(q * 2048 + 256 * h, 256), 256)] for h in range(8)]
@@ -118,6 +107,7 @@
             total = total + jnp.where(high == h, found[members * h : members * (h + 1)], 0.0)
         return total.astype(BF16)
 
+    smalls[0].wait()
     load.wait()
 
     def project_one(q, carry):
@@ -127,15 +117,15 @@
     lax.fori_loop(0, n, project_one, 0)
     pl.semaphore_wait(barrier, n + 1)
 
-    def state_copy(d):
+    def state_copy(d, h):
         q = peer(d)
-        return remote(band(pv, q), my_rows(state, p), in_s.at[d], in_r.at[d], member=q)
-
-    def send_state(pairs):
+        return remote(half_band(pv, q, h), my_rows(state.at[h], p), in_s.at[h, d], in_r.at[h, d], member=q)
+
+    def send_state(h, pairs):
         for k in pairs:
-            state_copy(k).start()
+            state_copy(k, h).start()
             if 2 * k != n:
-                state_copy(n - k).start()
+                state_copy(n - k, h).start()
 
     want_west = remote(want.at[pl.ds(0, 8)], asked.at[1], want_s.at[0], want_r.at[1], region=west)
     want_east = remote(want.at[pl.ds(16, 8)], asked.at[0], want_s.at[1], want_r.at[0], region=east)
@@ -149,12 +139,31 @@
         return carry
 
     lax.fori_loop(1, n, proj_send, 0)
+    send_state(0, range(1, 4))
+    blocks[1, pl.ds(pl.multiple_of(p * members, members), members), :] = psend[p]
+    owns = [
+        pltpu.make_async_copy(half_band(pv, p, h), my_rows(state.at[h], p), own_sem.at[h]) for h in range(2)
+    ]
+    for c in owns:
+        c.start()
+
+    for c in smalls[1:]:
+        c.wait()
+    data[0:32, :] = values[...].astype(F32)
+    data[32:64, :] = precisions[...].astype(F32)
+
+    slots = lookup.shape[-1]
+    named = lookup[0, pl.ds(p, 1), :]
+    side = lax.shift_right_logical(named, 12)
+    offset = (lax.shift_right_logical(named, 8) & 15) - p + 1
+    live = iota((1, slots), 1) < count[0, 0]
+    code = jnp.where(live, (dist[0] + 1).astype(F32), 0.0)
+    group = jnp.where(iota((32, slots), 0) == side * 8 + offset, code, 0.0).astype(BF16)
+    place = jnp.where(iota((256, slots), 0) == (named & 255), 1.0, 0.0).astype(BF16)
+    want[...] = dot(group, place, NT)
+
     want_west.start()
     want_east.start()
-    send_state((1, 2))
-    blocks[1, pl.ds(pl.multiple_of(p * members, members), members), :] = psend[p]
-    own = pltpu.make_async_copy(band(pv, p), my_rows(state, p), load_sem)
-    own.start()
 
     def proj_wait(d, carry):
         proj_copy(d).wait_recv()
@@ -165,7 +174,8 @@
     down = remote(blocks.at[1], blocks.at[2], halo_s.at[1], halo_r.at[1], member=peer(n - 1))
     up.start()
     down.start()
-    send_state((3, 4, 5, 6, 7, 8))
+    send_state(0, range(n // 2, 3, -1))
+    send_state(1, range(n // 2, 0, -1))
 
     departs, precision = [None] * 3, [None] * 3
 
@@ -270,11 +280,12 @@
         q = peer(d)
         return remote(my_rows(yf, q), my_rows(ye, q), y_s.at[d], y_r.at[d], region=west)
 
-    def east_send(d, carry):
-        east_copy(d).start()
-        return carry
-
-    lax.fori_loop(0, n, east_send, 0)
+    def east_send(i, carry):
+        east_copy(nth(i)).start()
+        return carry
+
+    lax.fori_loop(0, n - 1, east_send, 0)
+    east_copy(0).start()
     for side_, where in ((0, west), (1, east)):
         moment_copy(side_, where).wait_recv()
     gvec = gvec + (vr[0, 0:1, :] + vr[1, 0:1, :])
@@ -285,69 +296,74 @@
     factors = remote(fs, fe, f_s, f_r, region=west)
     factors.start()
 
-    own.wait()
-
-    def state_wait(d, carry):
-        state_copy(d).wait_recv()
-        return carry
-
-    lax.fori_loop(1, n, state_wait, 0)
     factors.wait_recv()
-    sums, bases, owns, easts = [], [], [], []
     tile = 512
     wide = jnp.concatenate(
         [split_rows(wbar), split_rows(fe[0:1, :]), jnp.ones((16, 512), BF16)], axis=0
     )
     totals = [jnp.sum(w, axis=1, keepdims=True) for w in (wbar, fe[0:1, :])]
-    for c in range(4):
-        cols = slice(tile * c, tile * (c + 1))
-        part = share[0, :, cols].astype(F32) * 0.125
-        rows = dot(wide, state[:, cols])
-        xbar = rows[32:33] * (1.0 / 512.0)
-        shifts = [
-            jnp.sum(rows[16 * k : 16 * (k + 1)], axis=0, keepdims=True) - totals[k] * xbar for k in range(2)
-        ]
-        sums.append(xbar)
-        bases.append(xbar + (1.0 - part) * shifts[0] + part * shifts[1])
-        owns.append((1.0 - part) * scale)
-        easts.append(part * fe[1:2, 0:tile])
-
-    def out_copy(d):
+
+    def out_copy(d, h):
         q = peer(d)
-        return remote(res.at[q], band(out, p), out_s.at[d], out_r.at[d], member=q)
-
-    def update(q):
-        at = pl.ds(pl.multiple_of(q * members, members), members)
-        lhs = jnp.concatenate([yf[at, :], ye[at, :]], axis=0)
-        weight = jnp.sum(lhs.astype(F32), axis=1, keepdims=True)
-        for c in range(4):
+        return remote(res.at[h, q], half_band(out, p, h), out_s.at[h, d], out_r.at[h, d], member=q)
+
+    mine = []
+    for h in range(2):
+        owns[h].wait()
+
+        def state_wait(d, carry):
+            state_copy(d, h).wait_recv()
+            return carry
+
+        lax.fori_loop(1, n, state_wait, 0)
+        rules = []
+        for c in range(2):
             cols = slice(tile * c, tile * (c + 1))
-            both = dot(lhs, state[:, cols]) - weight * sums[c]
-            value = bases[c] + owns[c] * both[:members] + easts[c] * both[members:]
-            res[q, :, cols] = value.astype(BF16)
-
-    def update_one(d, carry):
-        east_copy(d).wait_recv()
-        update(peer(d))
-        out_copy(d).start()
-        return carry
-
-    lax.fori_loop(1, n, update_one, 0)
-    east_copy(0).wait_recv()
-    update(p)
-    mine = pltpu.make_async_copy(res.at[p], band(out, p), load_sem)
-    mine.start()
+            part = share[0, :, 1024 * h + tile * c : 1024 * h + tile * (c + 1)].astype(F32) * 0.125
+            rows = dot(wide, state[h, :, cols])
+            xbar = rows[32:33] * (1.0 / 512.0)
+            shifts = [
+                jnp.sum(rows[16 * k : 16 * (k + 1)], axis=0, keepdims=True) - totals[k] * xbar
+                for k in range(2)
+            ]
+            base = xbar + (1.0 - part) * shifts[0] + part * shifts[1]
+            rules.append((cols, xbar, base, (1.0 - part) * scale, part * fe[1:2, 0:tile]))
+
+        def update(q):
+            at = pl.ds(pl.multiple_of(q * members, members), members)
+            lhs = jnp.concatenate([yf[at, :], ye[at, :]], axis=0)
+            weight = jnp.sum(lhs.astype(F32), axis=1, keepdims=True)
+            for cols, xbar, base, here, there in rules:
+                both = dot(lhs, state[h, :, cols]) - weight * xbar
+                res[h, q, :, cols] = (base + here * both[:members] + there * both[members:]).astype(BF16)
+
+        def update_one(i, carry):
+            d = nth(i)
+            if h == 0:
+                east_copy(d).wait_recv()
+            update(peer(d))
+            out_copy(d, h).start()
+            return carry
+
+        lax.fori_loop(0, n - 1, update_one, 0)
+        if h == 0:
+            east_copy(0).wait_recv()
+        update(p)
+        mine.append(pltpu.make_async_copy(res.at[h, p], half_band(out, p, h), own_sem.at[h]))
+        mine[h].start()
 
     def finish(d, carry):
-        out_copy(d).wait()
-        state_copy(d).wait_send()
+        for h in range(2):
+            out_copy(d, h).wait()
+            state_copy(d, h).wait_send()
         proj_copy(d).wait_send()
         east_copy(d).wait_send()
         return carry
 
     lax.fori_loop(1, n, finish, 0)
     east_copy(0).wait_send()
-    mine.wait()
+    for c in mine:
+        c.wait()
     for c in (want_west, want_east, up, down, factors):
         c.wait_send()
     for side_, where in ((0, west), (1, east)):
@@ -362,7 +378,7 @@
     members = prior.shape[0]
     return pl.pallas_call(
         functools.partial(kernel, n, regions),
-        out_shape=jax.ShapeDtypeStruct(prior.shape, BF16),
+        out_shape=pltpu.VMEM(prior.shape, BF16),
         in_specs=[hbm] * 7 + [pl.BlockSpec(memory_space=pltpu.SMEM)],
         out_specs=pl.BlockSpec(memory_space=pl.ANY),
         scratch_shapes=[
@@ -374,7 +390,7 @@
             pltpu.VMEM(dist.shape, jnp.int32),
             pltpu.VMEM(share.shape, jnp.int32),
             pltpu.VMEM(prior.shape, BF16),
-            pltpu.VMEM((512, 2048), BF16),
+            pltpu.VMEM((2, 512, 1024), BF16),
             pltpu.VMEM((n, members, 256), BF16),
             pltpu.VMEM((3, 512, 256), BF16),
             pltpu.VMEM((512, 768), BF16),
@@ -392,9 +408,9 @@
             pltpu.VMEM((512, 512), BF16),
             pltpu.VMEM((8, 512), F32),
             pltpu.VMEM((8, 512), F32),
-            pltpu.VMEM((n, members, 2048), BF16),
-            dma, dma((6,)),
-            dma((n,)), dma((n,)),
+            pltpu.VMEM((2, n, members, 1024), BF16),
+            dma, dma((6,)), dma((2,)),
+            dma((2, n)), dma((2, n)),
             dma((n,)), dma((n,)),
             dma((2,)), dma((2,)),
             dma((2,)), dma((2,)),
@@ -402,10 +418,10 @@
             dma((2,)), dma((2,)),
             dma((n,)), dma((n,)),
             dma, dma,
-            dma((n,)), dma((n,)),
+            dma((2, n)), dma((2, n)),
         ],
         compiler_params=pltpu.CompilerParams(
-            collective_id=0, has_side_effects=True, vmem_limit_bytes=63 * 1024 * 1024
+            collective_id=0, has_side_effects=True, vmem_limit_bytes=60 * 1024 * 1024
         ),
     )(prior, *(a.reshape(-1, 128) for a in (line, values, precision)), lookup, dist, share, count)
 

time: 120 us -> 115 us (0.958)
  Pallas kernels: 116 us -> 113 us
  local copies, waits for them, and re-layouts: 3.05 us -> 1.32 us
    pallas_call x1, Pallas kernels: 116 us -> 113 us  [local(): pl.pallas_call(functools.partial(kernel, n, regions), out_shape=pltpu.VME...]
    unnamed x1, local copies, waits for them, and re-layouts: 3.05 us -> 1.32 us
where the time goes in v3:
time: 115 us
  Pallas kernels  113 us (98%)
  local copies, waits for them, and re-layouts  1.32 us (1%)
    pallas_call x1, Pallas kernels, local(): pl.pallas_call(functools.partial(kernel, n, regions), out_shape=pltpu.VME...  113 us

profile of v3, /device:TPU:1, one launch (start us, length us, event | category | flops | bytes accessed | tf_op | source)
XLA Modules:
  0.0 114.6 jit_solution(6736607333704055647)
XLA Ops:
  0.7 112.6 %shard_map.82 = bf16[32,32768]{1,0:T(8,128)(2,1)S(1)} custom-call(bf16[32,32768]{1,0:T(8,128)(2,1)} %prior.1, s32[32,128]{1,0:T(8,128)} %bitcast.3, bf16[32,128]{1,0:T(8,128)(2,1)} %bitcast.4, bf16[32,128]{1,0:T(8,128)(2,1)} %bitcast.5, s32[1,16,1024]{2,1,0:T(8,128)} %lookup_in.1, s32[1,1,1024]{2,1,0:T(1,128)} %dist_in.1, s32[1,1,2048]{2,1,0:T(1,128)} %share_in.1, ...), custom_call_target="tpu_custom_call" | custom-call | tf_op jit(solution)/shard_map/pallas_call | solution.py:379
  113.2 1.3 %copy.10 = bf16[32,32768]{1,0:T(8,128)(2,1)} copy(bf16[32,32768]{1,0:T(8,128)(2,1)S(1)} %shard_map.82) | data formatting | bytes 4194304

commit v4 on v3

--- a/solution.py
+++ b/solution.py
@@ -352,24 +352,36 @@
         mine.append(pltpu.make_async_copy(res.at[h, p], half_band(out, p, h), own_sem.at[h]))
         mine[h].start()
 
-    def finish(d, carry):
-        for h in range(2):
-            out_copy(d, h).wait()
-            state_copy(d, h).wait_send()
+    def settle(d, carry):
         proj_copy(d).wait_send()
         east_copy(d).wait_send()
-        return carry
-
-    lax.fori_loop(1, n, finish, 0)
+        for h in range(2):
+            state_copy(d, h).wait_send()
+        return carry
+
+    lax.fori_loop(1, n, settle, 0)
     east_copy(0).wait_send()
-    for c in mine:
-        c.wait()
     for c in (want_west, want_east, up, down, factors):
         c.wait_send()
     for side_, where in ((0, west), (1, east)):
         moment_copy(side_, where).wait_send()
         for i in range(4):
             gram_copy(side_, i, where).wait_send()
+    for c in mine:
+        c.wait()
+
+    def leave(i, carry):
+        for h in range(2):
+            out_copy(nth(i), h).wait_send()
+        out_copy(nth(i), 0).wait_recv()
+        return carry
+
+    def arrive(i, carry):
+        out_copy(nth(i), 1).wait_recv()
+        return carry
+
+    lax.fori_loop(0, n - 1, leave, 0)
+    lax.fori_loop(0, n - 1, arrive, 0)
 
 
 def local(n, regions, prior, values, precision, line, lookup, count, dist, share):

time: 115 us -> 115 us (level)
  no operation moved by 1% of the time
where the time goes in v4:
time: 115 us; the launch traced here: 114 us
  Pallas kernels  112 us (97%)
  local copies, waits for them, and re-layouts  1.32 us (1%)
    pallas_call x1, Pallas kernels, local(): pl.pallas_call(functools.partial(kernel, n, regions), out_shape=pltpu.VME...  112 us

profile of v4, /device:TPU:1, one launch (start us, length us, event | category | flops | bytes accessed | tf_op | source)
XLA Modules:
  0.0 114.4 jit_solution(873886352952738336)
XLA Ops:
  0.7 112.4 %shard_map.82 = bf16[32,32768]{1,0:T(8,128)(2,1)S(1)} custom-call(bf16[32,32768]{1,0:T(8,128)(2,1)} %prior.1, s32[32,128]{1,0:T(8,128)} %bitcast.3, bf16[32,128]{1,0:T(8,128)(2,1)} %bitcast.4, bf16[32,128]{1,0:T(8,128)(2,1)} %bitcast.5, s32[1,16,1024]{2,1,0:T(8,128)} %lookup_in.1, s32[1,1,1024]{2,1,0:T(1,128)} %dist_in.1, s32[1,1,2048]{2,1,0:T(1,128)} %share_in.1, ...), custom_call_target="tpu_custom_call" | custom-call | tf_op jit(solution)/shard_map/pallas_call | solution.py:391
  113.0 1.3 %copy.10 = bf16[32,32768]{1,0:T(8,128)(2,1)} copy(bf16[32,32768]{1,0:T(8,128)(2,1)S(1)} %shard_map.82) | data formatting | bytes 4194304

commit v5 on v4

--- a/solution.py
+++ b/solution.py
@@ -175,7 +175,7 @@
     up.start()
     down.start()
     send_state(0, range(n // 2, 3, -1))
-    send_state(1, range(n // 2, 0, -1))
+    send_state(1, range(1, n // 2 + 1))
 
     departs, precision = [None] * 3, [None] * 3
 

time: 115 us -> 115 us (level)
  no operation moved by 1% of the time
where the time goes in v5:
time: 115 us
  Pallas kernels  113 us (98%)
  local copies, waits for them, and re-layouts  1.32 us (1%)
    pallas_call x1, Pallas kernels, local(): pl.pallas_call(functools.partial(kernel, n, regions), out_shape=pltpu.VME...  113 us

profile of v5, /device:TPU:1, one launch (start us, length us, event | category | flops | bytes accessed | tf_op | source)
XLA Modules:
  0.0 114.6 jit_solution(9835759906155505461)
XLA Ops:
  0.7 112.6 %shard_map.82 = bf16[32,32768]{1,0:T(8,128)(2,1)S(1)} custom-call(bf16[32,32768]{1,0:T(8,128)(2,1)} %prior.1, s32[32,128]{1,0:T(8,128)} %bitcast.3, bf16[32,128]{1,0:T(8,128)(2,1)} %bitcast.4, bf16[32,128]{1,0:T(8,128)(2,1)} %bitcast.5, s32[1,16,1024]{2,1,0:T(8,128)} %lookup_in.1, s32[1,1,1024]{2,1,0:T(1,128)} %dist_in.1, s32[1,1,2048]{2,1,0:T(1,128)} %share_in.1, ...), custom_call_target="tpu_custom_call" | custom-call | tf_op jit(solution)/shard_map/pallas_call | solution.py:391
  113.3 1.3 %copy.10 = bf16[32,32768]{1,0:T(8,128)(2,1)} copy(bf16[32,32768]{1,0:T(8,128)(2,1)S(1)} %shard_map.82) | data formatting | bytes 4194304
